TPU v7x, 32 devices: a whole 2x2x4 slice. The times are simulated.
32 devices in a mesh: lines: 2 (over y), freq: 8 (over z, x), rows: 2 (over core).
Axes of the slice: x: 2, y: 2, z: 4, core: 2. Of those that a mesh axis runs over, the one named last changes fastest.
Arguments:
- traces: float32 [1024, 512, 1024], P(('lines', 'freq'), 'rows'), parts along dimension 0, may hold values from -6 to 6
- win_start: int32 [1024], P(('lines', 'freq')), parts along dimension 0, may hold values from 0 to 255
- win_stop: int32 [1024], P(('lines', 'freq')), parts along dimension 0, may hold values from 768 to 1024
- shot_live: int32 [1024], P(('lines', 'freq')), parts along dimension 0, may hold values 0 or 1
- recv_live: int32 [1024], P(('lines', 'rows')), parts along dimension 0, may hold values 0 or 1
- band_start: int32 [2], P('lines'), parts along dimension 0, may hold values from 1 to 511
Outputs:
- multiples: bfloat16 [2, 16, 512, 512], P(None, ('lines', 'freq'), None, 'rows'), parts along dimension 1
There are 2 independent parts, one for each index of `lines`. A program takes and returns all parts, laid end to end along the dimension named above; each array names one. Nothing has to cross between parts.
All inputs are finite; a program needn't handle non-finite values. No bound on the sum of `shot_live` or of `recv_live` on one device may be relied on, other than what follows from the above.
Results may differ from a plain program's by a relative error of at most 0.001.
Values sent between devices are 32-bit elements; how exact they have to be, the bound alone decides.
A program may use at most 192 MiB of HBM per device.

v0:
```python
import math

import jax
import jax.numpy as jnp
from jax import lax
from jax.sharding import PartitionSpec as P

RAMP = 32
FDEV = 1


def dft_table(band_start, length, count):
    times = jnp.arange(length, dtype=jnp.int32)[None, :]
    freqs = (band_start[0] + jnp.arange(count, dtype=jnp.int32)[:, None]) % length
    phase = (freqs * times % length).astype(jnp.float32) * (2.0 * math.pi / length)
    return jnp.concatenate([jnp.cos(phase), -jnp.sin(phase)], 0) * (1.0 / math.sqrt(length))


def band_spectra(block, weight, live, table, count):
    tapered = block * weight[:, None, :] * live[:, :, None]
    flat = tapered.reshape(-1, block.shape[2])
    spec = lax.dot_general(table, flat, (((1,), (1,)), ((), ())), precision=lax.Precision.HIGHEST)
    return spec.reshape(2, count, block.shape[0], block.shape[1])


def shards(traces, win_start, win_stop, shot_live, recv_live, band_start):
    length = traces.shape[2]
    count = FDEV * lax.axis_size("freq")
    times = jnp.arange(length, dtype=jnp.float32)[None, :]
    start = win_start.astype(jnp.float32)[:, None]
    stop = win_stop.astype(jnp.float32)[:, None]
    weight = jnp.clip((times - start) / RAMP, 0.0, 1.0) * jnp.clip((stop - times) / RAMP, 0.0, 1.0)
    live = shot_live.astype(jnp.float32)[:, None] * recv_live.astype(jnp.float32)[None, :]
    table = dft_table(band_start, length, count)
    spec = band_spectra(traces, weight, live, table, count)
    local = lax.all_to_all(spec, "freq", split_axis=1, concat_axis=2, tiled=True)
    upper_limit = lax.Precision.HIGHEST
    piece = lax.all_gather(local, "rows", axis=3, tiled=True)
    re_re = jnp.einsum("wpn,wnb->wpb", piece[0], local[0], precision=upper_limit)
    im_im = jnp.einsum("wpn,wnb->wpb", piece[1], local[1], precision=upper_limit)
    re_im = jnp.einsum("wpn,wnb->wpb", piece[0], local[1], precision=upper_limit)
    im_re = jnp.einsum("wpn,wnb->wpb", piece[1], local[0], precision=upper_limit)
    product = jnp.stack([re_re - im_im, re_im + im_re])
    return (product * (1.0 / math.sqrt(local.shape[2]))).astype(jnp.bfloat16)


def solution(mesh):
    placed = (
        P(("lines", "freq"), "rows", None),
        P(("lines", "freq")),
        P(("lines", "freq")),
        P(("lines", "freq")),
        P(("lines", "rows")),
        P("lines"),
    )
    return jax.shard_map(
        shards,
        mesh=mesh,
        in_specs=placed,
        out_specs=P(None, ("lines", "freq"), None, "rows"),
        check_vma=False,
    )
```

profile of v0, /device:TPU:1, one launch (start us, length us, event | category | flops | bytes accessed | tf_op | source)
XLA Modules:
  0.0 126.1 jit_solution(11407299276474469210)
XLA Ops:
  6.5 0.0 all-gather.2.cloned.1.call-start
  7.2 0.7 convert_element_type.27
  7.9 0.7 convert_element_type.28
  8.5 0.7 convert_element_type.29
  9.2 0.7 convert_element_type.30
  9.9 0.2 fusion.22
  10.1 0.1 broadcast_multiply_fusion
  10.2 0.1 clamp_multiply_fusion
  10.3 58.9 %fusion = f32[2,8,64,256]{3,1,2,0:T(8,128)S(1)} fusion(f32[64,256,1024]{2,1,0:T(8,128)} %param.6, f32[64,256]{1,0:T(8,128)S(1)} %broadcast_multiply_fusion, f32[64,1024]{1,0:T(8,128)S(1)} %clamp_multiply_fusion, f32[8,1024]{1,0:T(8,128)S(1)} %get-tuple-element.8, f32[8,1024]{1,0:T(8,128)S(1)} %get-tuple-element.7), kind=kOutput, calls=%fused_computation | convolution fusion | flops 3254812672 | bytes 68550656 | tf_op jit(solution)/shard_map/dot_general | solution.py:22
  69.1 0.3 copy.10
  69.5 31.1 %all_to_all.12 = f32[2,8,64,256]{3,2,0,1:T(8,128)S(1)} all-to-all(f32[2,8,64,256]{3,2,0,1:T(8,128)S(1)} %copy.10), channel_id=1, replica_groups=mesh['lines'=2,'freq'=8,'rows'=2] {'freq'}, dimensions={1} | all-to-all | bytes 2097152 | tf_op jit(solution)/shard_map/all_to_all | solution.py:36
  100.6 1.1 copy.11
  101.7 0.0 all-gather.2.cloned.1.call-update
  101.7 0.1 fusion.26
  101.8 11.2 %all-gather.2.cloned.1.call-done = f32[2,1,512,512]{3,2,0,1:T(8,128)} async-done(((f32[2,1,512,256]{3,2,0,1:T(8,128)}), f32[2,1,512,512]{3,2,0,1:T(8,128)}) %all-gather.2.cloned.1.call-update) | async-done | bytes 2097168 | tf_op jit(solution)/shard_map/all_gather | solution.py:38
  113.0 0.0 copy-start
  113.0 2.4 %fusion.9 = f32[512,256]{1,0:T(8,128)S(1)} fusion(f32[512,256]{1,0:T(8,128)S(1)} %bitcast.31, f32[2,1,512,512]{3,2,0,1:T(8,128)} %all-gather.2.cloned.1.call-done), kind=kOutput, calls=%fused_computation.14 | convolution fusion | flops 805306368 | bytes 2097152 | tf_op jit(solution)/shard_map/wpn,wnb->wpb/dot_general | solution.py:41
  115.3 0.0 copy-done
  115.3 1.0 fusion.10
  116.3 1.0 fusion.6
  117.3 1.0 fusion.7
  118.3 0.9 fusion.8
  (1 shorter events, 0.0 us)
Async XLA Ops:
  6.5 106.4 %all-gather.2.cloned.1.call-start = ((), (), s32[]{:S(2)}) async-start(), calls=%async_computation.1 | async-start | bytes 3145728 | tf_op jit(solution)/shard_map/all_gather | solution.py:38
  113.0 2.4 %copy-start = (f32[2,1,512,512]{3,2,0,1:T(8,128)S(1)}, f32[2,1,512,512]{3,2,0,1:T(8,128)}, u32[]{:S(2)}) copy-start(f32[2,1,512,512]{3,2,0,1:T(8,128)} %all-gather.2.cloned.1.call-done) | copy-start | bytes 6291460
Sparse Core Ops, SparseCore 0:
  101.8 11.1 all-gather.1
where the time goes:
time: 126 us
  matrix products  64.2 us (51%)
  blocking collectives  31.1 us (25%)
  between operations  14.1 us (11%)
  waiting for transfers between devices  11.2 us (9%)
  other arithmetic  3.98 us (3%)
  local copies, waits for them, and re-layouts  1.53 us (1%)
    dot_general x1, matrix products, band_spectra(): lax.dot_general(table, flat, (((1,), (1,)), ((), ())), precision=lax.Prec...  58.9 us
    all_to_all x1, blocking collectives, shards(): lax.all_to_all(spec, 'freq', split_axis=1, concat_axis=2, tiled=True)  31.1 us
    all_gather x1, waiting for transfers between devices, shards(): piece = lax.all_gather(local, 'rows', axis=3, tiled=True)  11.2 us
  transfers between devices with their start and end apart: 1, of which 1 were waited for; matrix products, arithmetic and copies ran while one was open for 0% of the time, Pallas kernels for 0%

commit v1 on v0

v1 whole, which is shorter than its diff:
```python
import functools
import math

import jax
import jax.numpy as jnp
from jax import lax
from jax.experimental import pallas as pl
from jax.experimental.pallas import tpu as pltpu
from jax.sharding import PartitionSpec as P

RAMP = 32
SLOTS = 8
MESH = pl.DeviceIdType.MESH


def dft_table(band_start, length, count):
    times = jnp.arange(length, dtype=jnp.int32)[None, :]
    freqs = (band_start[0] + jnp.arange(count, dtype=jnp.int32)[:, None]) % length
    phase = (freqs * times % length).astype(jnp.float32) * (2.0 * math.pi / length)
    return jnp.concatenate([jnp.cos(phase), -jnp.sin(phase)], 0) * (1.0 / math.sqrt(length))


def split(x):
    high = x.astype(jnp.bfloat16)
    return high, (x - high.astype(jnp.float32)).astype(jnp.bfloat16)


def kernel(n, chunk, traces, weight, live, waves, out, table, slots, send, held, other, own, sib,
           slot_sem, send_sem, recv_sem, keep_sem, pass_sem, take_sem):
    me = lax.axis_index("freq")
    core = lax.axis_index("rows")
    shots, cols, length = traces.shape
    parts = shots // chunk

    def fetch(s):
        slot = lax.rem(s, SLOTS)
        return pltpu.make_async_copy(traces.at[s], slots.at[slot], slot_sem.at[slot])

    def remote(c, p):
        to = lax.rem(me + p, n)
        rows = pl.ds(c * chunk, chunk)
        return pltpu.make_async_remote_copy(
            send.at[:, to, rows, :], held.at[:, me, rows, :],
            send_sem.at[c, p - 1], recv_sem.at[c, p - 1],
            device_id={"freq": to}, device_id_type=MESH)

    def arrival(c, p):
        source = lax.rem(me + n - p, n)
        rows = pl.ds(c * chunk, chunk)
        return pltpu.make_async_remote_copy(
            send.at[:, source, rows, :], held.at[:, source, rows, :],
            send_sem.at[c, p - 1], recv_sem.at[c, p - 1],
            device_id={"freq": source}, device_id_type=MESH)

    def keep(c):
        rows = pl.ds(c * chunk, chunk)
        return pltpu.make_async_copy(send.at[:, me, rows, :], held.at[:, me, rows, :], keep_sem.at[c])

    def hand(c):
        rows = pl.ds(c * chunk, chunk)
        return pltpu.make_async_remote_copy(
            held.at[:, :, rows, :], other.at[:, :, rows, :], pass_sem.at[c], take_sem.at[c],
            device_id={"rows": 1 - core}, device_id_type=MESH)

    def hand_over(c):
        def land(p, carry):
            arrival(c, p).wait_recv()
            return carry
        lax.fori_loop(1, n, land, 0)
        keep(c).wait()
        hand(c).start()

    for s in range(min(SLOTS, shots)):
        fetch(s).start()

    table[:2 * n], table[2 * n:] = split(waves[...])

    barrier = pltpu.get_barrier_semaphore()

    def greet(p, carry):
        pl.semaphore_signal(barrier, inc=1, device_id={"freq": lax.rem(me + p, n)}, device_id_type=MESH)
        return carry
    lax.fori_loop(1, n, greet, 0)
    pl.semaphore_signal(barrier, inc=1, device_id={"rows": 1 - core}, device_id_type=MESH)

    def transform(s, carry):
        fetch(s).wait()
        slot = lax.rem(s, SLOTS)
        total = jnp.zeros((4 * n, cols), jnp.float32)
        step = 256
        for k in range(0, length, step):
            x = slots[slot, :, k:k + step] * weight[pl.ds(s, 1), k:k + step]
            high, low = split(x)
            part = table[:, k:k + step]
            for piece in (high, low):
                total += lax.dot_general(part, piece, (((1,), (1,)), ((), ())),
                                         preferred_element_type=jnp.float32)
        spec = (total[:2 * n] + total[2 * n:]) * live[...]
        for j in range(2 * n):
            send[j // n, j % n, pl.ds(s, 1), :] = spec[j:j + 1, :]

        @pl.when(s + SLOTS < shots)
        def _():
            fetch(s + SLOTS).start()
        return carry

    for c in range(parts):
        lax.fori_loop(c * chunk, (c + 1) * chunk, transform, 0)
        if c == 0:
            pl.semaphore_wait(barrier, n)

        def launch(p, carry):
            remote(c, p).start()
            return carry
        lax.fori_loop(1, n, launch, 0)
        keep(c).start()
        if c >= 2:
            hand_over(c - 2)
    for c in range(max(parts - 2, 0), parts):
        hand_over(c)

    def place(source_ref, target):
        for w in range(2):
            for source in range(n):
                target[w, source * shots:(source + 1) * shots, :] = source_ref[w, source]

    place(held, own)
    for c in range(parts):
        hand(c).wait_recv()
    place(other, sib)

    total_rows = n * shots
    scale = 1.0 / math.sqrt(total_rows)
    factors = []
    for half in (core, 1 - core):
        start = pl.multiple_of(half * cols, cols)
        right = jnp.concatenate([own[w, pl.ds(start, cols), :] for w in range(2)], 1)
        factors.append(split(right))
    tile = 128

    def multiply(i, carry):
        rows = pl.ds(pl.multiple_of(i * tile, tile), tile)
        sums = []
        for w in range(2):
            acc = jnp.zeros((tile, 2 * cols), jnp.float32)
            for ref, (right_high, right_low) in zip((own, sib), factors):
                high, low = split(ref[w, rows, :])
                acc += jnp.dot(high, right_high, preferred_element_type=jnp.float32)
                acc += jnp.dot(high, right_low, preferred_element_type=jnp.float32)
                acc += jnp.dot(low, right_high, preferred_element_type=jnp.float32)
            sums.append(acc)
        out[0, rows, :] = ((sums[0][:, :cols] - sums[1][:, cols:]) * scale).astype(out.dtype)
        out[1, rows, :] = ((sums[0][:, cols:] + sums[1][:, :cols]) * scale).astype(out.dtype)
        return carry
    lax.fori_loop(0, total_rows // tile, multiply, 0)

    for c in range(parts):
        def sent(p, carry):
            remote(c, p).wait_send()
            return carry
        lax.fori_loop(1, n, sent, 0)
        hand(c).wait_send()


def shards(traces, win_start, win_stop, shot_live, recv_live, band_start):
    shots, cols, length = traces.shape
    n = lax.axis_size("freq")
    times = jnp.arange(length, dtype=jnp.float32)[None, :]
    start = win_start.astype(jnp.float32)[:, None]
    stop = win_stop.astype(jnp.float32)[:, None]
    weight = jnp.clip((times - start) / RAMP, 0.0, 1.0) * jnp.clip((stop - times) / RAMP, 0.0, 1.0)
    weight = weight * shot_live.astype(jnp.float32)[:, None]
    waves = dft_table(band_start, length, n)
    chunk = min(16, shots)
    parts = shots // chunk
    block = (2, n, shots, cols)
    vmem = pl.BlockSpec(memory_space=pltpu.VMEM)
    out = pl.pallas_call(
        functools.partial(kernel, n, chunk),
        out_shape=jax.ShapeDtypeStruct((2, n * shots, cols), jnp.bfloat16),
        in_specs=[pl.BlockSpec(memory_space=pl.ANY), vmem, vmem, vmem],
        out_specs=vmem,
        scratch_shapes=[
            pltpu.VMEM((4 * n, length), jnp.bfloat16),
            pltpu.VMEM((SLOTS, cols, length), jnp.float32),
            pltpu.VMEM(block, jnp.float32),
            pltpu.VMEM(block, jnp.float32),
            pltpu.VMEM(block, jnp.float32),
            pltpu.VMEM((2, n * shots, cols), jnp.float32),
            pltpu.VMEM((2, n * shots, cols), jnp.float32),
            pltpu.SemaphoreType.DMA((SLOTS,)),
            pltpu.SemaphoreType.DMA((parts, n - 1)),
            pltpu.SemaphoreType.DMA((parts, n - 1)),
            pltpu.SemaphoreType.DMA((parts,)),
            pltpu.SemaphoreType.DMA((parts,)),
            pltpu.SemaphoreType.DMA((parts,)),
        ],
        compiler_params=pltpu.CompilerParams(
            collective_id=0, has_side_effects=True, vmem_limit_bytes=56 * 1024 * 1024),
        cost_estimate=pl.CostEstimate(flops=2 * 10**10, bytes_accessed=4 * shots * cols * length, transcendentals=0),
    )(traces, weight, recv_live.astype(jnp.float32)[None, :], waves)
    return out[:, None]


def solution(mesh):
    placed = (
        P(("lines", "freq"), "rows", None),
        P(("lines", "freq")),
        P(("lines", "freq")),
        P(("lines", "freq")),
        P(("lines", "rows")),
        P("lines"),
    )
    return jax.shard_map(
        shards,
        mesh=mesh,
        in_specs=placed,
        out_specs=P(None, ("lines", "freq"), None, "rows"),
        check_vma=False,
    )
```

time: 126 us -> 52.8 us (0.42)
  matrix products: 64.2 us -> 0 us
  Pallas kernels: 0 us -> 45.1 us
  blocking collectives: 31.1 us -> 0 us
  between operations: 14.1 us -> 0.67 us
  waiting for transfers between devices: 11.2 us -> 0 us
    dot_general x5 -> x0, matrix products: 64.2 us -> none  [the longest x1 58.9 us: band_spectra(): lax.dot_general(table, flat, (((1,), (1,)), ((), ())), precision=lax.Prec...]
    pallas_call x0 -> x1, Pallas kernels: none -> 45.1 us  [shards(): pl.pallas_call(functools.partial(kernel, n, chunk), out_shape=jax.ShapeDt...]
    all_to_all x1 -> x0, blocking collectives: 31.1 us -> none  [shards(): lax.all_to_all(spec, 'freq', split_axis=1, concat_axis=2, tiled=True)]
    all_gather x1 -> x0, waiting for transfers between devices: 11.2 us -> none  [shards(): piece = lax.all_gather(local, 'rows', axis=3, tiled=True)]
    unnamed x2 -> x1, local copies, waits for them, and re-layouts: 0.01 us -> 1.87 us
    mul x2, other arithmetic: 0.21 us -> 1.49 us  [the longest x1 0.84 us: shards(): weight = weight * shot_live.astype(jnp.float32)[:, None]]
  transfers between devices with their start and end apart: 1 -> 0, of which waited for: 1 -> 0; matrix products, arithmetic and copies ran while one was open for 0% -> 0% of each run, Pallas kernels for 0% -> 0%
where the time goes in v1:
time: 52.8 us; the launch traced here: 52.6 us
  Pallas kernels  45.1 us (85%)
  other arithmetic  4.94 us (9%)
  local copies, waits for them, and re-layouts  1.87 us (4%)
  between operations  0.67 us (1%)
    pallas_call x1, Pallas kernels, shards(): pl.pallas_call(functools.partial(kernel, n, chunk), out_shape=jax.ShapeDt...  45.1 us
    unnamed x1, local copies, waits for them, and re-layouts  1.87 us
    convert_element_type x1, other arithmetic, shards(): recv_live.astype(jnp.float32)[None, :]  1.25 us

profile of v1, /device:TPU:1, one launch (start us, length us, event | category | flops | bytes accessed | tf_op | source)
XLA Modules:
  0.0 52.6 jit_solution(11349192063108831445)
XLA Ops:
  0.7 0.7 %convert_element_type.15 = f32[64]{0:T(128)S(1)} convert(s32[64]{0:T(128)} %param.7) | non-fusion elementwise | flops 64 | bytes 512 | tf_op jit(solution)/shard_map/convert_element_type | solution.py:169
  1.3 0.7 %convert_element_type.16 = f32[64]{0:T(128)S(1)} convert(s32[64]{0:T(128)} %param.8) | non-fusion elementwise | flops 64 | bytes 512 | tf_op jit(solution)/shard_map/convert_element_type | solution.py:170
  2.0 0.7 %convert_element_type.17 = f32[64]{0:T(128)S(1)} convert(s32[64]{0:T(128)} %param.9) | non-fusion elementwise | flops 64 | bytes 512 | tf_op jit(solution)/shard_map/convert_element_type | solution.py:172
  2.6 1.3 %convert_element_type.18 = f32[256]{0:T(256)} convert(s32[256]{0:T(256)} %param.10) | non-fusion elementwise | flops 256 | bytes 2048 | tf_op jit(solution)/shard_map/convert_element_type | solution.py:201
  3.9 0.2 fusion.6
  4.1 0.6 %maximum_multiply_fusion.waves = f32[16,1024]{1,0:T(8,128)} fusion(f32[8,1024]{1,0:T(8,128)S(1)} %get-tuple-element.6, f32[8,1024]{1,0:T(8,128)S(1)} %get-tuple-element.5), kind=kLoop, calls=%fused_computation.1 | loop fusion | flops 32768 | bytes 131072 | tf_op jit(solution)/shard_map/mul | solution.py:20
  4.8 0.8 %multiply_multiply_fusion.weight = f32[64,1024]{1,0:T(8,128)} fusion(f32[64]{0:T(128)S(1)} %convert_element_type.17, f32[64]{0:T(128)S(1)} %convert_element_type.16, f32[64]{0:T(128)S(1)} %convert_element_type.15), kind=kLoop, calls=%fused_computation | loop fusion | flops 524288 | bytes 262912 | tf_op jit(solution)/shard_map/mul | solution.py:172
  5.6 45.1 %shard_map.64 = bf16[2,512,256]{2,1,0:T(8,128)(2,1)} custom-call(f32[64,256,1024]{2,1,0:T(8,128)} %traces.1, f32[64,1024]{1,0:T(8,128)} %multiply_multiply_fusion.weight, f32[1,256]{1,0:T(1,128)} %bitcast.7, f32[16,1024]{1,0:T(8,128)} %maximum_multiply_fusion.waves), custom_call_target="tpu_custom_call" | custom-call | flops 20000000000 | bytes 67108864 | tf_op jit(solution)/shard_map/pallas_call | solution.py:178
  50.7 1.9 %copy.10 = bf16[2,1,512,256]{3,2,1,0:T(8,128)(2,1)} copy(bf16[2,1,512,256]{3,2,1,0:T(8,128)(2,1)} %bitcast.6) | data formatting | bytes 1048576
  (1 shorter events, 0.0 us)

commit v2 on v1

--- a/solution.py
+++ b/solution.py
@@ -13,19 +13,12 @@
 MESH = pl.DeviceIdType.MESH
 
 
-def dft_table(band_start, length, count):
-    times = jnp.arange(length, dtype=jnp.int32)[None, :]
-    freqs = (band_start[0] + jnp.arange(count, dtype=jnp.int32)[:, None]) % length
-    phase = (freqs * times % length).astype(jnp.float32) * (2.0 * math.pi / length)
-    return jnp.concatenate([jnp.cos(phase), -jnp.sin(phase)], 0) * (1.0 / math.sqrt(length))
-
-
 def split(x):
     high = x.astype(jnp.bfloat16)
     return high, (x - high.astype(jnp.float32)).astype(jnp.bfloat16)
 
 
-def kernel(n, chunk, traces, weight, live, waves, out, table, slots, send, held, other, own, sib,
+def kernel(n, chunk, traces, win_start, win_stop, shot_live, recv_live, band_start, out, waves, slots, send, held, other, own, sib,
            slot_sem, send_sem, recv_sem, keep_sem, pass_sem, take_sem):
     me = lax.axis_index("freq")
     core = lax.axis_index("rows")
@@ -73,7 +66,14 @@
     for s in range(min(SLOTS, shots)):
         fetch(s).start()
 
-    table[:2 * n], table[2 * n:] = split(waves[...])
+    row = lax.broadcasted_iota(jnp.int32, (2 * n, length), 0)
+    times = lax.broadcasted_iota(jnp.int32, (2 * n, length), 1)
+    sine = row >= n
+    freqs = (band_start[0] + row - jnp.where(sine, n, 0)) & (length - 1)
+    turns = (freqs * times + jnp.where(sine, length // 4, 0)) & (length - 1)
+    waves[...] = jnp.cos(turns.astype(jnp.float32) * (2.0 * math.pi / length)) * (1.0 / math.sqrt(length))
+    live = recv_live[...].astype(jnp.float32)
+    clock = lax.broadcasted_iota(jnp.int32, (1, length), 1)
 
     barrier = pltpu.get_barrier_semaphore()
 
@@ -87,15 +87,17 @@
         fetch(s).wait()
         slot = lax.rem(s, SLOTS)
         total = jnp.zeros((4 * n, cols), jnp.float32)
+        rise = jnp.clip((clock - win_start[s]).astype(jnp.float32) * (1.0 / RAMP), 0.0, 1.0)
+        fall = jnp.clip((win_stop[s] - clock).astype(jnp.float32) * (1.0 / RAMP), 0.0, 1.0)
+        weight = rise * fall * shot_live[s].astype(jnp.float32)
+        table = jnp.concatenate(split(waves[...] * weight), 0)
         step = 256
         for k in range(0, length, step):
-            x = slots[slot, :, k:k + step] * weight[pl.ds(s, 1), k:k + step]
-            high, low = split(x)
             part = table[:, k:k + step]
-            for piece in (high, low):
+            for piece in split(slots[slot, :, k:k + step]):
                 total += lax.dot_general(part, piece, (((1,), (1,)), ((), ())),
                                          preferred_element_type=jnp.float32)
-        spec = (total[:2 * n] + total[2 * n:]) * live[...]
+        spec = (total[:2 * n] + total[2 * n:]) * live
         for j in range(2 * n):
             send[j // n, j % n, pl.ds(s, 1), :] = spec[j:j + 1, :]
 
@@ -165,23 +167,18 @@
 def shards(traces, win_start, win_stop, shot_live, recv_live, band_start):
     shots, cols, length = traces.shape
     n = lax.axis_size("freq")
-    times = jnp.arange(length, dtype=jnp.float32)[None, :]
-    start = win_start.astype(jnp.float32)[:, None]
-    stop = win_stop.astype(jnp.float32)[:, None]
-    weight = jnp.clip((times - start) / RAMP, 0.0, 1.0) * jnp.clip((stop - times) / RAMP, 0.0, 1.0)
-    weight = weight * shot_live.astype(jnp.float32)[:, None]
-    waves = dft_table(band_start, length, n)
-    chunk = min(16, shots)
+    chunk = min(8, shots)
     parts = shots // chunk
     block = (2, n, shots, cols)
     vmem = pl.BlockSpec(memory_space=pltpu.VMEM)
+    smem = pl.BlockSpec(memory_space=pltpu.SMEM)
     out = pl.pallas_call(
         functools.partial(kernel, n, chunk),
         out_shape=jax.ShapeDtypeStruct((2, n * shots, cols), jnp.bfloat16),
-        in_specs=[pl.BlockSpec(memory_space=pl.ANY), vmem, vmem, vmem],
+        in_specs=[pl.BlockSpec(memory_space=pl.ANY), smem, smem, smem, vmem, smem],
         out_specs=vmem,
         scratch_shapes=[
-            pltpu.VMEM((4 * n, length), jnp.bfloat16),
+            pltpu.VMEM((2 * n, length), jnp.float32),
             pltpu.VMEM((SLOTS, cols, length), jnp.float32),
             pltpu.VMEM(block, jnp.float32),
             pltpu.VMEM(block, jnp.float32),
@@ -198,7 +195,7 @@
         compiler_params=pltpu.CompilerParams(
             collective_id=0, has_side_effects=True, vmem_limit_bytes=56 * 1024 * 1024),
         cost_estimate=pl.CostEstimate(flops=2 * 10**10, bytes_accessed=4 * shots * cols * length, transcendentals=0),
-    )(traces, weight, recv_live.astype(jnp.float32)[None, :], waves)
+    )(traces, win_start, win_stop, shot_live, recv_live[None, :], band_start)
     return out[:, None]
 
 

time: 52.8 us -> 46.7 us (0.88)
  other arithmetic: 4.94 us -> 0 us
  Pallas kernels: 45.1 us -> 44 us
    convert_element_type x4 -> x0, other arithmetic: 3.23 us -> none  [the longest x1 1.25 us: shards(): recv_live.astype(jnp.float32)[None, :]]
    mul x2 -> x0, other arithmetic: 1.49 us -> none  [the longest x1 0.84 us: shards(): weight = weight * shot_live.astype(jnp.float32)[:, None]]
    pallas_call x1, Pallas kernels: 45.1 us -> 44 us  [shards(): pl.pallas_call(functools.partial(kernel, n, chunk), out_shape=jax.ShapeDt...]
where the time goes in v2:
time: 46.7 us; the launch traced here: 46.5 us
  Pallas kernels  44 us (94%)
  local copies, waits for them, and re-layouts  1.87 us (4%)
  between operations  0.66 us (1%)
    pallas_call x1, Pallas kernels, shards(): pl.pallas_call(functools.partial(kernel, n, chunk), out_shape=jax.ShapeDt...  44 us
    unnamed x1, local copies, waits for them, and re-layouts  1.87 us

profile of v2, /device:TPU:1, one launch (start us, length us, event | category | flops | bytes accessed | tf_op | source)
XLA Modules:
  0.0 46.5 jit_solution(13818843690488756720)
XLA Ops:
  0.7 44.0 %shard_map.64 = bf16[2,512,256]{2,1,0:T(8,128)(2,1)} custom-call(f32[64,256,1024]{2,1,0:T(8,128)} %traces.1, s32[64]{0:T(128)} %win_start.1, s32[64]{0:T(128)} %win_stop.1, s32[64]{0:T(128)} %shot_live.1, s32[1,256]{1,0:T(1,128)} %bitcast.5, s32[1]{0:T(128)S(6)} %copy.9.band_start), custom_call_target="tpu_custom_call" | custom-call | flops 20000000000 | bytes 67108864 | tf_op jit(solution)/shard_map/pallas_call | solution.py:175
  44.6 1.9 %copy.10 = bf16[2,1,512,256]{3,2,1,0:T(8,128)(2,1)} copy(bf16[2,1,512,256]{3,2,1,0:T(8,128)(2,1)} %bitcast.4) | data formatting | bytes 1048576

commit v3 on v2

--- a/solution.py
+++ b/solution.py
@@ -10,6 +10,7 @@
 
 RAMP = 32
 SLOTS = 8
+LAG = 3
 MESH = pl.DeviceIdType.MESH
 
 
@@ -111,14 +112,14 @@
         if c == 0:
             pl.semaphore_wait(barrier, n)
 
-        def launch(p, carry):
-            remote(c, p).start()
+        def launch(i, carry):
+            remote(c, lax.rem(i - 1 + core * (n // 2 - 1), n - 1) + 1).start()
             return carry
         lax.fori_loop(1, n, launch, 0)
         keep(c).start()
-        if c >= 2:
-            hand_over(c - 2)
-    for c in range(max(parts - 2, 0), parts):
+        if c >= LAG:
+            hand_over(c - LAG)
+    for c in range(max(parts - LAG, 0), parts):
         hand_over(c)
 
     def place(source_ref, target):

time: 46.7 us -> 47.1 us (level)
  no operation moved by 1% of the time
where the time goes in v3:
time: 47.1 us; the launch traced here: 46.9 us
  Pallas kernels  44.3 us (94%)
  local copies, waits for them, and re-layouts  1.87 us (4%)
  between operations  0.66 us (1%)
    pallas_call x1, Pallas kernels, shards(): pl.pallas_call(functools.partial(kernel, n, chunk), out_shape=jax.ShapeDt...  44.3 us
    unnamed x1, local copies, waits for them, and re-layouts  1.87 us

profile of v3, /device:TPU:1, one launch (start us, length us, event | category | flops | bytes accessed | tf_op | source)
XLA Modules:
  0.0 46.9 jit_solution(15589830558858819144)
XLA Ops:
  0.7 44.3 %shard_map.64 = bf16[2,512,256]{2,1,0:T(8,128)(2,1)} custom-call(f32[64,256,1024]{2,1,0:T(8,128)} %traces.1, s32[64]{0:T(128)} %win_start.1, s32[64]{0:T(128)} %win_stop.1, s32[64]{0:T(128)} %shot_live.1, s32[1,256]{1,0:T(1,128)} %bitcast.5, s32[1]{0:T(128)S(6)} %copy.9.band_start), custom_call_target="tpu_custom_call" | custom-call | flops 20000000000 | bytes 67108864 | tf_op jit(solution)/shard_map/pallas_call | solution.py:176
  45.0 1.9 %copy.10 = bf16[2,1,512,256]{3,2,1,0:T(8,128)(2,1)} copy(bf16[2,1,512,256]{3,2,1,0:T(8,128)(2,1)} %bitcast.4) | data formatting | bytes 1048576
